TPU v7x, 128 devices: a whole 4x4x4 slice. The times are simulated.
128 devices in a mesh: pair: 4 (over y), db: 32 (over x, z, core).
Axes of the slice: x: 4, y: 4, z: 4, core: 2. Of those that a mesh axis runs over, the one named last changes fastest.
Arguments:
- forward_strain: bfloat16 [4, 2048, 6, 8192], P('pair', 'db'), may hold values from -6 to 6
- backward_strain: bfloat16 [4, 2048, 6, 8192], P('pair', 'db'), may hold values from -6 to 6
- request_point: int32 [32, 32, 8], P('db'), may hold values from 0 to 63
- node_slot: int32 [2, 8, 16384], P(None, None, 'db'), may hold values from 0 to 255, as said below
- node_weight: float32 [2, 8, 16384], P(None, None, 'db'), may hold values from 0.05 to 0.25
- band_filter: float32 [16, 512], replicated, may hold values from 0.1 to 1
- misfit: float32 [32, 16], replicated, may hold values from 0.1 to 1
- pair_group: int32 [32], replicated, may hold values from 0 to 3, as said below
Outputs:
- kernel: float32 [16, 16384], P('pair', 'db')
Inputs may be any that keep to these rules, and one draw needn't show every extreme that they name: For each w, all 8 nodes of one inversion point come from one database device; the forward device and the backward device of a point always differ. node_slot = d * 8 + c, where c is below the number of slots that d fills for the point's owner, which is 1 to 8. The last database device fills 8 slots for every owner, and one owner receives 8 slots from every database device. Slots that no node names may hold any local point. `pair_group`: each group holds exactly 8 station pairs.
All inputs are finite; a program needn't handle non-finite values.
Results may differ from a plain program's by a relative error of at most 0.0052.
Values may be sent and summed in bfloat16 or wider, within the bound.
A program may use at most 128 MiB of HBM per device.

v0:
```python
import functools
import math

import jax
import jax.numpy as jnp
import ml_dtypes
import numpy as np
from jax import lax
from jax.experimental import pallas as pl
from jax.experimental.pallas import tpu as pltpu
from jax.sharding import PartitionSpec as P

MESH = pl.DeviceIdType.MESH
f32, bf16, i32 = jnp.float32, jnp.bfloat16, jnp.int32

SIDE = 4
CHIPS = SIDE * SIDE
PLANES = 4
LAG = 4


def table(steps, freqs, total):
    turn = (np.arange(steps)[:, None] * freqs[None, :] % total).astype(np.float32)
    angle = turn * np.float32(2.0 * math.pi / total)
    blocks = (len(freqs) // 64, 64)
    cos = np.cos(angle).reshape((steps,) + blocks)
    sin = -np.sin(angle).reshape((steps,) + blocks)
    both = np.stack([cos, sin], axis=2)
    return both.reshape(steps, 2 * len(freqs)).astype(ml_dtypes.bfloat16)


def tables(steps, count):
    even = np.stack([table(steps // 4, np.arange(r, count, 4), steps) for r in (0, 2)])
    odd = table(steps // 2, np.arange(1, count, 2), steps)
    return even, odd


def body(
    fs, bs, even_hbm, odd_hbm, slot, weight, request, band, misfit, group, out,
    xin, even, odd, fold_even, fold_odd, snd0, snd1, got0, got1, nodef, node, quads, sib, onehot, mix, rows, cross,
    bandx, rss, rsr,
    x_sem, t_sem, nd_s, nd_r, q_s, q_r, a_s, a_r, f_s, f_r, sb_s, sb_r, rs_s, rs_r, plane_sem,
):
    y = lax.axis_index("pair")
    d = lax.axis_index("db")
    core = d % 2
    chip = d // 2
    cx, cz = chip // SIDE, chip % SIDE
    snds, gots = (snd0, snd1), (got0, got1)

    def hop(a):
        return (2 + 3 * a + 3 * (a * (a - 1) // 2)) % SIDE

    def chip_to(i):
        return ((cx + hop(i // SIDE)) % SIDE) * SIDE + (cz + hop(i % SIDE)) % SIDE

    def chip_from(i):
        return ((cx + SIDE - hop(i // SIDE)) % SIDE) * SIDE + (cz + SIDE - hop(i % SIDE)) % SIDE

    sibling = (y, chip * 2 + 1 - core)

    def remote(src, dst, s, r, dev):
        return pltpu.make_async_remote_copy(
            src_ref=src, dst_ref=dst, send_sem=s, recv_sem=r, device_id=dev, device_id_type=MESH
        )

    def strain_load(slab):
        t, w, h = slab // 4, slab // 2 % 2, slab % 2
        return pltpu.make_async_copy((fs, bs)[w].at[t + 3 * h], xin.at[slab], x_sem.at[slab])

    even_load = pltpu.make_async_copy(even_hbm, even, t_sem.at[0])
    odd_load = pltpu.make_async_copy(odd_hbm, odd, t_sem.at[1])
    for slab in range(4):
        strain_load(slab).start()
    even_load.start()
    odd_load.start()
    for slab in range(4, 12):
        strain_load(slab).start()

    barrier = pltpu.get_barrier_semaphore()

    @pl.loop(0, CHIPS - 1)
    def _(i):
        pl.semaphore_signal(barrier, inc=1, device_id=(y, chip_to(i) * 2 + core), device_id_type=MESH)

    for step in range(1, PLANES):
        pl.semaphore_signal(barrier, inc=1, device_id=((y + step) % PLANES, d), device_id_type=MESH)
    pl.semaphore_signal(barrier, inc=1, device_id=sibling, device_id_type=MESH)

    points = slot.shape[2]
    nodef[...] = jnp.zeros_like(nodef)
    for w in (0, 1):
        slots = slot[w]
        weights = weight[w]
        place = slots % 8
        which = lax.broadcasted_iota(i32, (8, points), 0)
        by_slot = jnp.zeros((8, points), f32)
        for k in range(8):
            by_slot += jnp.where(which == place[k : k + 1], weights[k : k + 1], 0.0)
        source = (slots[0:1] // 8).astype(f32)
        for q in range(PLANES):
            span = slice(128 * q, 128 * q + 128)
            own = jnp.where(y == q, 1.0, 0.0)
            nodef[8 * w : 8 * w + 8, :] += by_slot[:, span] * own
            nodef[16 + 4 * w + q : 17 + 4 * w + q, :] = source[:, span]
    lane = lax.broadcasted_iota(i32, (8, 256), 1)
    spread = (lane % 8 == lax.broadcasted_iota(i32, (8, 256), 0)).astype(f32)
    spread_out = lax.dot_general(
        request[...].astype(f32), spread, (((0,), (0,)), ((), ())), preferred_element_type=f32
    )
    owner = lax.broadcasted_iota(i32, (32, 256), 0)
    lane = lax.broadcasted_iota(i32, (32, 256), 1)
    for k in (0, 1):
        keep = (owner == 2 * (lane // 16) + k) & ((lane // 8) % 2 == core)
        row = jnp.sum(jnp.where(keep, spread_out, 0.0), axis=0, keepdims=True)
        for q in (0, 1):
            nodef[24 + 2 * k + q : 25 + 2 * k + q, :] = row[:, 128 * q : 128 * q + 128]
    node[chip] = nodef[...].astype(bf16)

    def node_copy(i):
        return remote(node.at[chip], node.at[chip], nd_s, nd_r, (y, chip_to(i) * 2 + core))

    def quad_copy(step):
        return remote(node.at[:, 0:16], quads.at[y], q_s, q_r, ((y + step) % PLANES, d))

    local = xin.shape[1]
    steps = xin.shape[2]
    quarter = steps // 4
    rescale = steps ** (-0.5)
    width = 256

    def part_copy(part, i):
        to = chip_to(i)
        return remote(
            snds[part].at[to], gots[part].at[chip, core], a_s.at[part], a_r.at[part, i], (y, to * 2 + core)
        )

    def part_forward(part, i, of):
        s = chip_from(i)
        return remote(
            gots[part].at[s, core], gots[part].at[s, of], f_s.at[part], f_r.at[part, i], sibling
        )

    def spectra(t, part, place, pairs):
        @pl.loop(0, 4)
        def _(r):
            slab = 4 * t + r
            pltpu.make_async_copy(fs.at[0], xin.at[slab], x_sem.at[slab]).wait()

            @pl.loop(0, quarter // width)
            def _(n):
                at = pl.multiple_of(n * width, width)
                x0, x1, x2, x3 = (xin[slab, :, pl.ds(at + q * quarter, width)].astype(f32) for q in range(4))
                a, b = x0 + x2, x1 + x3
                span = pl.ds(r * local, local)
                fold_even[0, span, pl.ds(at, width)] = (a + b).astype(bf16)
                fold_even[1, span, pl.ds(at, width)] = (a - b).astype(bf16)
                fold_odd[span, pl.ds(at, width)] = (x0 - x2).astype(bf16)
                fold_odd[span, pl.ds(at + quarter, width)] = (x1 - x3).astype(bf16)

        if t == 0:
            even_load.wait()
            odd_load.wait()
        for n in range(4):
            if n < 2:
                sums = jnp.dot(fold_even[n], even[n], preferred_element_type=f32)
            else:
                sums = jnp.dot(fold_odd[...], odd[:, (n - 2) * 256 : (n - 1) * 256], preferred_element_type=f32)
            sums = (sums * rescale).astype(bf16)
            for u in (0, 1):
                for r in range(4):
                    at = 128 * ((r // 2) * pairs + place)
                    snds[part][4 * n + 2 * u + r % 2, :, at : at + 128] = sums[
                        r * local : (r + 1) * local, 128 * u : 128 * u + 128
                    ]

    def depart(part):
        @pl.loop(0, CHIPS - 1)
        def _(i):
            part_copy(part, i).start()

        gots[part][chip, core] = snds[part][chip]
        part_forward(part, CHIPS - 1, core).start()

    spectra(0, 0, 0, 2)
    spectra(1, 0, 1, 2)

    pl.semaphore_wait(barrier, CHIPS - 1 + 1 + PLANES - 1)

    for step in range(1, PLANES):
        pl.semaphore_signal(plane_sem, inc=1, device_id=((y + step) % PLANES, d), device_id_type=MESH)

    @pl.loop(0, CHIPS - 1)
    def _(i):
        node_copy(i).start()

    depart(0)
    spectra(2, 1, 0, 1)
    depart(1)

    remote(node.at[0:15], node.at[0:15], nd_s, nd_r, sibling).wait_recv()
    sib_copy = remote(node.at[:, 16:32], sib, sb_s, sb_r, sibling)
    sib_copy.start()
    for step in range(1, PLANES):
        quad_copy(step).start()
    quads[y] = node[:, 0:16]

    count = band.shape[1]
    freq = lax.broadcasted_iota(i32, (count, 128), 0)
    at = lax.broadcasted_iota(i32, (count, 128), 1) % 64
    block = chip // 2
    even_freq = 4 * (64 * (block % 2) + at) + 2 * (block // 2)
    odd_freq = 2 * (64 * (block % 4) + at) + 1
    pick = (freq == jnp.where(block < 4, even_freq, odd_freq)).astype(f32)
    chosen = jnp.dot(band[...], pick, precision=lax.Precision.HIGHEST, preferred_element_type=f32)
    own_group = (group[...] == y).astype(f32)
    group_weight = jnp.sum(misfit[...] * own_group, axis=1, keepdims=True)
    component_scale = jnp.where(chip % 2 == 0, 1.0, 2.0)
    chosen = chosen * group_weight * (component_scale * count ** (-0.5))
    high = chosen.astype(bf16).astype(f32)
    low = chosen - high
    bandx[...] = jnp.concatenate(
        [jnp.concatenate([high, high], axis=1), jnp.concatenate([low, jnp.zeros_like(low)], axis=1)], axis=0
    ).astype(bf16)

    sib_copy.wait_recv()

    @pl.loop(0, CHIPS)
    def _(s):
        mine = node[s, 16:32].astype(f32)
        theirs = sib[s].astype(f32)
        for q in (0, 1):
            mine_row = jnp.where(core == 0, mine[8 + q : 9 + q], mine[10 + q : 11 + q])
            their_row = jnp.where(core == 0, theirs[8 + q : 9 + q], theirs[10 + q : 11 + q])
            lane = lax.broadcasted_iota(i32, (128, 128), 1)
            place = lax.broadcasted_iota(i32, (128, 128), 0).astype(f32)
            wanted = mine_row + their_row + 64.0 * ((lane // 8) % 2).astype(f32)
            hits = jnp.where(place == wanted, 1.0, 0.0)
            onehot[s, 128 * q : 128 * q + 128, :] = hits.T.astype(bf16)

    remote(quads.at[0:3], quads.at[0:3], q_s, q_r, sibling).wait_recv()

    @pl.loop(0, CHIPS)
    def _(o):
        sources = node[o, 16:32].astype(f32)
        for q in range(PLANES):
            quad = quads[q, o].astype(f32)
            for w in (0, 1):
                by_slot = quad[8 * w : 8 * w + 8]
                source = sources[4 * w + q : 4 * w + q + 1]
                for e in range(CHIPS):
                    two = [jnp.where(source == float(2 * e + k), by_slot, 0.0) for k in (0, 1)]
                    mix[o, w, 16 * e : 16 * e + 16, 128 * q : 128 * q + 128] = jnp.concatenate(
                        two, axis=0
                    ).astype(bf16)

    def receive(part, i):
        part_copy(part, i).wait_recv()
        part_forward(part, i, core).start()

    def gather(part, i):
        s = chip_from(i)
        part_forward(part, i, 1 - core).wait_recv()
        at = pl.ds(pl.multiple_of(s * 16, 16), 16)
        lanes = gots[part].shape[3]
        for n in range(lanes // 256):
            found = gots[part][s, :, :, 256 * n : 256 * n + 256].reshape(2 * local, 256)
            taken = jnp.dot(onehot[s], found, preferred_element_type=f32)
            rows[:, at, 512 * part + 256 * n : 512 * part + 256 * n + 256] = (
                taken.reshape(CHIPS, 16, 256).astype(bf16)
            )

    @pl.loop(0, CHIPS - 1 + LAG)
    def _(i):
        @pl.when(i < CHIPS - 1)
        def _():
            receive(0, i)

        @pl.when(i >= LAG)
        def _():
            gather(0, i - LAG)

    gather(0, CHIPS - 1)

    over_slots = (((0,), (0,)), ((), ()))

    def mixed(o, w, lanes):
        return lax.dot_general(rows[o, :, lanes], mix[o, w], over_slots, preferred_element_type=f32)

    @pl.loop(0, CHIPS, step=2)
    def _(o):
        receive(1, o)

        @pl.when(o < CHIPS - 2)
        def _():
            receive(1, o + 1)

        for e in (0, 1):
            product = mixed(o + e, 0, slice(0, 256)) * mixed(o + e, 1, slice(256, 512))
            cross[o + e] = product[0:128] + product[128:256]

        @pl.when(o >= LAG)
        def _():
            gather(1, o - LAG)
            gather(1, o + 1 - LAG)

    @pl.loop(CHIPS - LAG, CHIPS)
    def _(i):
        gather(1, i)

    pl.semaphore_wait(plane_sem, PLANES - 1)

    def sum_copy(i, step):
        to = chip_to(i)
        p = (y + step) % PLANES
        return remote(rss.at[to * PLANES + p], rsr.at[i * PLANES + step], rs_s, rs_r, (p, to * 2 + core))

    @pl.loop(0, CHIPS, step=2)
    def _(first):
        for e in (0, 1):
            o = chip_to(first + e)
            total = cross[o] + mixed(o, 0, slice(512, 640)) * mixed(o, 1, slice(640, 768))
            high = total.astype(bf16)
            low = (total - high.astype(f32)).astype(bf16)
            banded = jnp.dot(bandx[...], jnp.concatenate([high, low], axis=0), preferred_element_type=f32)
            banded = banded[0:16] + banded[16:32]
            for p in range(PLANES):
                pieces = [banded[4 * p : 4 * p + 4, 128 * q : 128 * q + 128] for q in range(points // 128)]
                rss[o * PLANES + p] = jnp.concatenate(pieces, axis=0).astype(bf16)
        for e in (0, 1):
            for step in (2, 1, 3):
                sum_copy(first + e, step).start()
        sum_copy(first, 0).start()

        @pl.when(first < CHIPS - 2)
        def _():
            sum_copy(first + 1, 0).start()

    own = (CHIPS - 1) * PLANES
    rsr[own] = rss[chip * PLANES + y]
    remote(rss.at[0:63], rsr.at[0:63], rs_s, rs_r, sibling).wait_recv()

    summed = jnp.sum(rsr[...].astype(f32), axis=0)
    for q in range(points // 128):
        out[:, 128 * q : 128 * q + 128] = summed[4 * q : 4 * q + 4]

    sib_copy.wait_send()
    remote(node.at[0:15], node.at[0:15], nd_s, nd_r, sibling).wait_send()
    remote(quads.at[0:3], quads.at[0:3], q_s, q_r, sibling).wait_send()
    remote(rss.at[0:63], rsr.at[0:63], rs_s, rs_r, sibling).wait_send()
    for part in (0, 1):
        sent, came = snds[part], gots[part]
        remote(sent.at[0:15], sent.at[0:15], a_s.at[part], a_r.at[part, 0], sibling).wait_send()
        remote(came.at[:, core], came.at[:, core], f_s.at[part], f_r.at[part, 0], sibling).wait_send()


def per_device(even, odd, fwd, bwd, request, slot, weight, band, misfit, group):
    comps, local, steps = fwd.shape[2], fwd.shape[1], fwd.shape[3]
    points = slot.shape[2]
    bands, count = band.shape
    args = (
        jnp.transpose(fwd[0], (1, 0, 2)),
        jnp.transpose(bwd[0], (1, 0, 2)),
        even,
        odd,
        slot,
        weight,
        jnp.transpose(request[0], (1, 0)),
        band,
        jnp.transpose(misfit, (1, 0)),
        group[None, :],
    )
    vmem = pl.BlockSpec(memory_space=pltpu.VMEM)
    hbm = pl.BlockSpec(memory_space=pltpu.HBM)
    dma = pltpu.SemaphoreType.DMA
    return pl.pallas_call(
        body,
        out_shape=jax.ShapeDtypeStruct((bands // 4, points), f32),
        in_specs=[hbm] * 4 + [vmem] * 6,
        out_specs=vmem,
        scratch_shapes=[
            pltpu.VMEM((12, local, steps), bf16),
            pltpu.VMEM(even.shape, bf16),
            pltpu.VMEM(odd.shape, bf16),
            pltpu.VMEM((2, 4 * local, steps // 4), bf16),
            pltpu.VMEM((4 * local, steps // 2), bf16),
            pltpu.VMEM((CHIPS, local, 512), bf16),
            pltpu.VMEM((CHIPS, local, 256), bf16),
            pltpu.VMEM((CHIPS, 2, local, 512), bf16),
            pltpu.VMEM((CHIPS, 2, local, 256), bf16),
            pltpu.VMEM((32, 128), f32),
            pltpu.VMEM((CHIPS, 32, 128), bf16),
            pltpu.VMEM((PLANES, CHIPS, 16, 128), bf16),
            pltpu.VMEM((CHIPS, 16, 128), bf16),
            pltpu.VMEM((CHIPS, 256, 2 * local), bf16),
            pltpu.VMEM((CHIPS, 2, 256, points), bf16),
            pltpu.VMEM((CHIPS, 256, 768), bf16),
            pltpu.VMEM((CHIPS, 128, points), f32),
            pltpu.VMEM((2 * bands, 256), bf16),
            pltpu.VMEM((CHIPS * PLANES, 16, 128), bf16),
            pltpu.VMEM((CHIPS * PLANES, 16, 128), bf16),
            dma((12,)),
            dma((2,)),
            dma,
            dma,
            dma,
            dma,
            dma((2,)),
            dma((2, CHIPS)),
            dma((2,)),
            dma((2, CHIPS)),
            dma,
            dma,
            dma,
            dma,
            pltpu.SemaphoreType.REGULAR,
        ],
        compiler_params=pltpu.CompilerParams(
            collective_id=0, has_side_effects=True, vmem_limit_bytes=60 * 2**20
        ),
    )(*args)


def solution(mesh):
    even, odd = tables(8192, 512)
    in_specs = (
        P(),
        P(),
        P("pair", "db", None, None),
        P("pair", "db", None, None),
        P("db", None, None),
        P(None, None, "db"),
        P(None, None, "db"),
        P(),
        P(),
        P(),
    )
    inner = jax.shard_map(
        per_device, mesh=mesh, in_specs=in_specs, out_specs=P("pair", "db"), check_vma=False
    )
    return lambda *args: inner(jnp.asarray(even), jnp.asarray(odd), *args)
```

profile of v0, /device:TPU:1, one launch (start us, length us, event | category | flops | bytes accessed | tf_op | source)
XLA Modules:
  0.0 59.3 jit_solution(14386445932661045709)
XLA Ops:
  0.0 58.0 %shard_map.100 = f32[4,512]{1,0:T(4,128)} custom-call(bf16[6,64,8192]{2,1,0:T(8,128)(2,1)} %bitcast.11, bf16[6,64,8192]{2,1,0:T(8,128)(2,1)} %bitcast.12, bf16[2,2048,256]{2,1,0:T(8,128)(2,1)} %constant.4.clone.even_hbm, bf16[4096,512]{1,0:T(8,128)(2,1)} %constant.5.clone.odd_hbm, s32[2,8,512]{2,1,0:T(8,128)} %slot.1, f32[2,8,512]{2,1,0:T(8,128)} %weight.1, ...), custom_call_target="tpu_custom_call" | custom-call | tf_op jit(solution)/shard_map/pallas_call | solution.py:376
  58.0 1.3 %copy.12 = f32[4,512]{1,0:T(4,128)} copy(f32[4,512]{1,0:T(4,128)} %shard_map.100) | data formatting | bytes 16384
where the time goes:
time: 59.5 us; the launch traced here: 59.3 us
  Pallas kernels  58 us (97%)
  local copies, waits for them, and re-layouts  1.3 us (2%)
    pallas_call x1, Pallas kernels, per_device(): pl.pallas_call(body, out_shape=jax.ShapeDtypeStruct((bands // 4, points),...  58 us
    unnamed x1, local copies, waits for them, and re-layouts  1.3 us

commit v1 on v0

v1 whole, which is shorter than its diff:
```python
import functools
import math

import jax
import jax.numpy as jnp
import ml_dtypes
import numpy as np
from jax import lax
from jax.experimental import pallas as pl
from jax.experimental.pallas import tpu as pltpu
from jax.sharding import PartitionSpec as P

MESH = pl.DeviceIdType.MESH
f32, bf16, i32 = jnp.float32, jnp.bfloat16, jnp.int32

SIDE = 4
CHIPS = SIDE * SIDE
PLANES = 4
PARTS = 3


def table(steps, freqs, total):
    turn = (np.arange(steps)[:, None] * freqs[None, :] % total).astype(np.float32)
    angle = turn * np.float32(2.0 * math.pi / total)
    blocks = (len(freqs) // 64, 64)
    cos = np.cos(angle).reshape((steps,) + blocks)
    sin = -np.sin(angle).reshape((steps,) + blocks)
    both = np.stack([cos, sin], axis=2)
    return both.reshape(steps, 2 * len(freqs)).astype(ml_dtypes.bfloat16)


def tables(steps, count):
    even = np.stack([table(steps // 4, np.arange(r, count, 4), steps) for r in (0, 2)])
    odd = table(steps // 2, np.arange(1, count, 2), steps)
    return even, odd


def body(
    fs, bs, even_hbm, odd_hbm, slot, weight, request, band, misfit, group, out,
    xin, even, odd, fold_even, fold_odd, snd, got, nodef, node, quads, sib, onehot, mix, rows, cross,
    bandx, rss, rsr,
    x_sem, t_sem, nd_s, nd_r, q_s, q_r, a_s, a_r, f_s, f_r, sb_s, sb_r, rs_s, rs_r, plane_sem,
):
    y = lax.axis_index("pair")
    d = lax.axis_index("db")
    core = d % 2
    chip = d // 2
    cx, cz = chip // SIDE, chip % SIDE

    def hop(a):
        return 2 + 3 * a + 3 * (a * (a - 1) // 2)

    def row_to(a):
        return lax.rem(cx + hop(a), SIDE) * SIDE

    def row_from(a):
        return lax.rem(cx + 9 * SIDE - hop(a), SIDE) * SIDE

    order = (2, 1, 3, 0)
    z_to = [lax.rem(cz + h, SIDE) for h in order]
    z_from = [lax.rem(cz + SIDE - h, SIDE) for h in order]

    def others(act):
        @pl.loop(0, SIDE)
        def _(a):
            for b in range(SIDE - 1):
                act(a, b)

            @pl.when(a < SIDE - 1)
            def _():
                act(a, SIDE - 1)

    sibling = (y, chip * 2 + 1 - core)

    def remote(src, dst, s, r, dev):
        return pltpu.make_async_remote_copy(
            src_ref=src, dst_ref=dst, send_sem=s, recv_sem=r, device_id=dev, device_id_type=MESH
        )

    def strain_load(slab):
        t, w, h = slab // 4, slab // 2 % 2, slab % 2
        return pltpu.make_async_copy((fs, bs)[w].at[t + 3 * h], xin.at[slab], x_sem.at[slab])

    even_load = pltpu.make_async_copy(even_hbm, even, t_sem.at[0])
    odd_load = pltpu.make_async_copy(odd_hbm, odd, t_sem.at[1])
    for slab in range(4):
        strain_load(slab).start()
    even_load.start()
    odd_load.start()

    barrier = pltpu.get_barrier_semaphore()

    others(
        lambda a, b: pl.semaphore_signal(
            barrier, inc=1, device_id=(y, (row_to(a) + z_to[b]) * 2 + core), device_id_type=MESH
        )
    )
    for step in range(1, PLANES):
        pl.semaphore_signal(barrier, inc=1, device_id=((y + step) % PLANES, d), device_id_type=MESH)
    pl.semaphore_signal(barrier, inc=1, device_id=sibling, device_id_type=MESH)

    def node_copy(a, b):
        return remote(node.at[chip], node.at[chip], nd_s, nd_r, (y, (row_to(a) + z_to[b]) * 2 + core))

    def quad_copy(step):
        return remote(node.at[:, 0:16], quads.at[y], q_s, q_r, ((y + step) % PLANES, d))

    local = xin.shape[1]
    steps = xin.shape[2]
    quarter = steps // 4
    rescale = steps ** (-0.5)
    width = 256

    def part_copy(part, a, b):
        to = row_to(a) + z_to[b]
        return remote(
            snd.at[part, to], got.at[part, chip, core], a_s.at[part], a_r.at[part, a, b], (y, to * 2 + core)
        )

    def part_forward(part, a, b, of):
        s = row_from(a) + z_from[b]
        return remote(got.at[part, s, core], got.at[part, s, of], f_s.at[part], f_r.at[part, a, b], sibling)

    def spectra(t):
        @pl.loop(0, 4)
        def _(r):
            slab = 4 * t + r
            pltpu.make_async_copy(fs.at[0], xin.at[slab], x_sem.at[slab]).wait()

            @pl.loop(0, quarter // width)
            def _(n):
                at = pl.multiple_of(n * width, width)
                x0, x1, x2, x3 = (xin[slab, :, pl.ds(at + q * quarter, width)].astype(f32) for q in range(4))
                a, b = x0 + x2, x1 + x3
                span = pl.ds(r * local, local)
                fold_even[0, span, pl.ds(at, width)] = (a + b).astype(bf16)
                fold_even[1, span, pl.ds(at, width)] = (a - b).astype(bf16)
                fold_odd[span, pl.ds(at, width)] = (x0 - x2).astype(bf16)
                fold_odd[span, pl.ds(at + quarter, width)] = (x1 - x3).astype(bf16)

        if t < PARTS - 1:
            for slab in range(4 * t + 4, 4 * t + 8):
                strain_load(slab).start()
        if t == 0:
            even_load.wait()
            odd_load.wait()
        for n in range(4):
            if n < 2:
                sums = jnp.dot(fold_even[n], even[n], preferred_element_type=f32)
            else:
                sums = jnp.dot(fold_odd[...], odd[:, (n - 2) * 256 : (n - 1) * 256], preferred_element_type=f32)
            sums = (sums * rescale).astype(bf16)
            for u in (0, 1):
                for r in range(4):
                    at = 128 * (r // 2)
                    snd[t, 4 * n + 2 * u + r % 2, :, at : at + 128] = sums[
                        r * local : (r + 1) * local, 128 * u : 128 * u + 128
                    ]

    def depart(part):
        others(lambda a, b: part_copy(part, a, b).start())
        got[part, chip, core] = snd[part, chip]
        part_forward(part, SIDE - 1, SIDE - 1, core).start()

    spectra(0)

    points = slot.shape[2]
    nodef[...] = jnp.zeros_like(nodef)
    for w in (0, 1):
        slots = slot[w]
        weights = weight[w]
        place = slots % 8
        which = lax.broadcasted_iota(i32, (8, points), 0)
        by_slot = jnp.zeros((8, points), f32)
        for k in range(8):
            by_slot += jnp.where(which == place[k : k + 1], weights[k : k + 1], 0.0)
        source = (slots[0:1] // 8).astype(f32)
        for q in range(PLANES):
            span = slice(128 * q, 128 * q + 128)
            own = jnp.where(y == q, 1.0, 0.0)
            nodef[8 * w : 8 * w + 8, :] += by_slot[:, span] * own
            nodef[16 + 4 * w + q : 17 + 4 * w + q, :] = source[:, span]
    lane = lax.broadcasted_iota(i32, (8, 256), 1)
    spread = (lane % 8 == lax.broadcasted_iota(i32, (8, 256), 0)).astype(f32)
    spread_out = lax.dot_general(
        request[...].astype(f32), spread, (((0,), (0,)), ((), ())), preferred_element_type=f32
    )
    owner = lax.broadcasted_iota(i32, (32, 256), 0)
    lane = lax.broadcasted_iota(i32, (32, 256), 1)
    for k in (0, 1):
        keep = (owner == 2 * (lane // 16) + k) & ((lane // 8) % 2 == core)
        row = jnp.sum(jnp.where(keep, spread_out, 0.0), axis=0, keepdims=True)
        for q in (0, 1):
            nodef[24 + 2 * k + q : 25 + 2 * k + q, :] = row[:, 128 * q : 128 * q + 128]
    node[chip] = nodef[...].astype(bf16)

    pl.semaphore_wait(barrier, CHIPS - 1 + 1 + PLANES - 1)

    for step in range(1, PLANES):
        pl.semaphore_signal(plane_sem, inc=1, device_id=((y + step) % PLANES, d), device_id_type=MESH)

    others(lambda a, b: node_copy(a, b).start())
    depart(0)
    spectra(1)
    depart(1)
    spectra(2)
    depart(2)

    remote(node.at[0:15], node.at[0:15], nd_s, nd_r, sibling).wait_recv()
    sib_copy = remote(node.at[:, 16:32], sib, sb_s, sb_r, sibling)
    sib_copy.start()
    for step in range(1, PLANES):
        quad_copy(step).start()
    quads[y] = node[:, 0:16]

    count = band.shape[1]
    freq = lax.broadcasted_iota(i32, (count, 128), 0)
    at = lax.broadcasted_iota(i32, (count, 128), 1) % 64
    block = chip // 2
    even_freq = 4 * (64 * (block % 2) + at) + 2 * (block // 2)
    odd_freq = 2 * (64 * (block % 4) + at) + 1
    pick = (freq == jnp.where(block < 4, even_freq, odd_freq)).astype(f32)
    chosen = jnp.dot(band[...], pick, precision=lax.Precision.HIGHEST, preferred_element_type=f32)
    own_group = (group[...] == y).astype(f32)
    group_weight = jnp.sum(misfit[...] * own_group, axis=1, keepdims=True)
    component_scale = jnp.where(chip % 2 == 0, 1.0, 2.0)
    chosen = chosen * group_weight * (component_scale * count ** (-0.5))
    high = chosen.astype(bf16).astype(f32)
    low = chosen - high
    bandx[...] = jnp.concatenate(
        [jnp.concatenate([high, high], axis=1), jnp.concatenate([low, jnp.zeros_like(low)], axis=1)], axis=0
    ).astype(bf16)

    sib_copy.wait_recv()

    @pl.loop(0, CHIPS)
    def _(s):
        mine = node[s, 16:32].astype(f32)
        theirs = sib[s].astype(f32)
        for q in (0, 1):
            mine_row = jnp.where(core == 0, mine[8 + q : 9 + q], mine[10 + q : 11 + q])
            their_row = jnp.where(core == 0, theirs[8 + q : 9 + q], theirs[10 + q : 11 + q])
            lane = lax.broadcasted_iota(i32, (128, 128), 1)
            place = lax.broadcasted_iota(i32, (128, 128), 0).astype(f32)
            wanted = mine_row + their_row + 64.0 * ((lane // 8) % 2).astype(f32)
            hits = jnp.where(place == wanted, 1.0, 0.0)
            onehot[s, 128 * q : 128 * q + 128, :] = hits.T.astype(bf16)

    def receive(part, a):
        def one(b):
            part_copy(part, a, b).wait_recv()
            part_forward(part, a, b, core).start()

        for b in range(SIDE - 1):
            one(b)

        @pl.when(a < SIDE - 1)
        def _():
            one(SIDE - 1)

    def gather(part, a):
        for b in range(SIDE):
            part_forward(part, a, b, 1 - core).wait_recv()
        for b in range(SIDE):
            s = row_from(a) + z_from[b]
            at = pl.ds(pl.multiple_of(s * 16, 16), 16)
            found = got[part, s].reshape(2 * local, 256)
            taken = jnp.dot(onehot[s], found, preferred_element_type=f32)
            rows[:, at, 256 * part : 256 * part + 256] = taken.reshape(CHIPS, 16, 256).astype(bf16)

    @pl.loop(0, SIDE + 1)
    def _(a):
        @pl.when(a < SIDE)
        def _():
            receive(0, a)

        @pl.when(a >= 1)
        def _():
            gather(0, a - 1)

    remote(quads.at[0:3], quads.at[0:3], q_s, q_r, sibling).wait_recv()

    @pl.loop(0, CHIPS)
    def _(o):
        sources = node[o, 16:32].astype(f32)
        for q in range(PLANES):
            quad = quads[q, o].astype(f32)
            for w in (0, 1):
                by_slot = quad[8 * w : 8 * w + 8]
                source = sources[4 * w + q : 4 * w + q + 1]
                for e in range(CHIPS):
                    two = [jnp.where(source == float(2 * e + k), by_slot, 0.0) for k in (0, 1)]
                    mix[o, w, 16 * e : 16 * e + 16, 128 * q : 128 * q + 128] = jnp.concatenate(
                        two, axis=0
                    ).astype(bf16)

    over_slots = (((0,), (0,)), ((), ()))

    def mixed(o, w, part):
        at = 256 * part + 128 * w
        return lax.dot_general(rows[o, :, at : at + 128], mix[o, w], over_slots, preferred_element_type=f32)

    for part in (0, 1):
        @pl.loop(0, SIDE)
        def _(a):
            receive(part + 1, a)
            for e in range(SIDE):
                o = SIDE * a + e
                product = mixed(o, 0, part) * mixed(o, 1, part)
                cross[o] = product if part == 0 else cross[o] + product

        @pl.loop(0, SIDE)
        def _(a):
            gather(part + 1, a)

    pl.semaphore_wait(plane_sem, PLANES - 1)

    def sum_copy(a, b, step):
        to = row_to(a) + z_to[b]
        p = (y + step) % PLANES
        at = (SIDE * a + b) * PLANES + step
        return remote(rss.at[to * PLANES + p], rsr.at[at], rs_s, rs_r, (p, to * 2 + core))

    @pl.loop(0, SIDE)
    def _(a):
        for pair in (0, 2):
            for b in (pair, pair + 1):
                o = row_to(a) + z_to[b]
                total = cross[o] + mixed(o, 0, 2) * mixed(o, 1, 2)
                high = total.astype(bf16)
                low = (total - high.astype(f32)).astype(bf16)
                banded = jnp.dot(bandx[...], jnp.concatenate([high, low], axis=0), preferred_element_type=f32)
                banded = banded[0:16] + banded[16:32]
                for p in range(PLANES):
                    pieces = [banded[4 * p : 4 * p + 4, 128 * q : 128 * q + 128] for q in range(points // 128)]
                    rss[o * PLANES + p] = jnp.concatenate(pieces, axis=0).astype(bf16)
            for b in (pair, pair + 1):
                for step in (2, 1, 3):
                    sum_copy(a, b, step).start()
            sum_copy(a, pair, 0).start()
            if pair == 0:
                sum_copy(a, 1, 0).start()
            else:

                @pl.when(a < SIDE - 1)
                def _():
                    sum_copy(a, 3, 0).start()

    own = (CHIPS - 1) * PLANES
    rsr[own] = rss[chip * PLANES + y]
    remote(rss.at[0:63], rsr.at[0:63], rs_s, rs_r, sibling).wait_recv()

    summed = jnp.sum(rsr[...].astype(f32), axis=0)
    for q in range(points // 128):
        out[:, 128 * q : 128 * q + 128] = summed[4 * q : 4 * q + 4]

    sib_copy.wait_send()
    remote(node.at[0:15], node.at[0:15], nd_s, nd_r, sibling).wait_send()
    remote(quads.at[0:3], quads.at[0:3], q_s, q_r, sibling).wait_send()
    remote(rss.at[0:63], rsr.at[0:63], rs_s, rs_r, sibling).wait_send()
    for part in range(PARTS):
        sent, came = snd.at[part, 0:15], got.at[part, :, core]
        remote(sent, sent, a_s.at[part], a_r.at[part, 0, 0], sibling).wait_send()
        remote(came, came, f_s.at[part], f_r.at[part, 0, 0], sibling).wait_send()


def per_device(even, odd, fwd, bwd, request, slot, weight, band, misfit, group):
    comps, local, steps = fwd.shape[2], fwd.shape[1], fwd.shape[3]
    points = slot.shape[2]
    bands, count = band.shape
    args = (
        jnp.transpose(fwd[0], (1, 0, 2)),
        jnp.transpose(bwd[0], (1, 0, 2)),
        even,
        odd,
        slot,
        weight,
        jnp.transpose(request[0], (1, 0)),
        band,
        jnp.transpose(misfit, (1, 0)),
        group[None, :],
    )
    vmem = pl.BlockSpec(memory_space=pltpu.VMEM)
    hbm = pl.BlockSpec(memory_space=pltpu.HBM)
    dma = pltpu.SemaphoreType.DMA
    return pl.pallas_call(
        body,
        out_shape=jax.ShapeDtypeStruct((bands // 4, points), f32),
        in_specs=[hbm] * 4 + [vmem] * 6,
        out_specs=vmem,
        scratch_shapes=[
            pltpu.VMEM((12, local, steps), bf16),
            pltpu.VMEM(even.shape, bf16),
            pltpu.VMEM(odd.shape, bf16),
            pltpu.VMEM((2, 4 * local, steps // 4), bf16),
            pltpu.VMEM((4 * local, steps // 2), bf16),
            pltpu.VMEM((PARTS, CHIPS, local, 256), bf16),
            pltpu.VMEM((PARTS, CHIPS, 2, local, 256), bf16),
            pltpu.VMEM((32, 128), f32),
            pltpu.VMEM((CHIPS, 32, 128), bf16),
            pltpu.VMEM((PLANES, CHIPS, 16, 128), bf16),
            pltpu.VMEM((CHIPS, 16, 128), bf16),
            pltpu.VMEM((CHIPS, 256, 2 * local), bf16),
            pltpu.VMEM((CHIPS, 2, 256, points), bf16),
            pltpu.VMEM((CHIPS, 256, 768), bf16),
            pltpu.VMEM((CHIPS, 128, points), f32),
            pltpu.VMEM((2 * bands, 256), bf16),
            pltpu.VMEM((CHIPS * PLANES, 16, 128), bf16),
            pltpu.VMEM((CHIPS * PLANES, 16, 128), bf16),
            dma((12,)),
            dma((2,)),
            dma,
            dma,
            dma,
            dma,
            dma((PARTS,)),
            dma((PARTS, SIDE, SIDE)),
            dma((PARTS,)),
            dma((PARTS, SIDE, SIDE)),
            dma,
            dma,
            dma,
            dma,
            pltpu.SemaphoreType.REGULAR,
        ],
        compiler_params=pltpu.CompilerParams(
            collective_id=0, has_side_effects=True, vmem_limit_bytes=60 * 2**20
        ),
    )(*args)


def solution(mesh):
    even, odd = tables(8192, 512)
    in_specs = (
        P(),
        P(),
        P("pair", "db", None, None),
        P("pair", "db", None, None),
        P("db", None, None),
        P(None, None, "db"),
        P(None, None, "db"),
        P(),
        P(),
        P(),
    )
    inner = jax.shard_map(
        per_device, mesh=mesh, in_specs=in_specs, out_specs=P("pair", "db"), check_vma=False
    )
    return lambda *args: inner(jnp.asarray(even), jnp.asarray(odd), *args)
```

time: 59.5 us -> 48.4 us (0.81)
  Pallas kernels: 58 us -> 46.8 us
    pallas_call x1, Pallas kernels: 58 us -> 46.8 us  [per_device(): pl.pallas_call(body, out_shape=jax.ShapeDtypeStruct((bands // 4, points),...]
where the time goes in v1:
time: 48.4 us; the launch traced here: 48.1 us
  Pallas kernels  46.8 us (97%)
  local copies, waits for them, and re-layouts  1.3 us (3%)
    pallas_call x1, Pallas kernels, per_device(): pl.pallas_call(body, out_shape=jax.ShapeDtypeStruct((bands // 4, points),...  46.8 us
    unnamed x1, local copies, waits for them, and re-layouts  1.3 us

profile of v1, /device:TPU:1, one launch (start us, length us, event | category | flops | bytes accessed | tf_op | source)
XLA Modules:
  0.0 48.1 jit_solution(5017393401534104435)
XLA Ops:
  0.0 46.8 %shard_map.100 = f32[4,512]{1,0:T(4,128)} custom-call(bf16[6,64,8192]{2,1,0:T(8,128)(2,1)} %bitcast.11, bf16[6,64,8192]{2,1,0:T(8,128)(2,1)} %bitcast.12, bf16[2,2048,256]{2,1,0:T(8,128)(2,1)} %constant.4.clone.even_hbm, bf16[4096,512]{1,0:T(8,128)(2,1)} %constant.5.clone.odd_hbm, s32[2,8,512]{2,1,0:T(8,128)} %slot.1, f32[2,8,512]{2,1,0:T(8,128)} %weight.1, ...), custom_call_target="tpu_custom_call" | custom-call | tf_op jit(solution)/shard_map/pallas_call | solution.py:386
  46.8 1.3 %copy.12 = f32[4,512]{1,0:T(4,128)} copy(f32[4,512]{1,0:T(4,128)} %shard_map.100) | data formatting | bytes 16384

commit v2 on v1

--- a/solution.py
+++ b/solution.py
@@ -59,6 +59,8 @@
     order = (2, 1, 3, 0)
     z_to = [lax.rem(cz + h, SIDE) for h in order]
     z_from = [lax.rem(cz + SIDE - h, SIDE) for h in order]
+    z_db = [z * 2 + core for z in z_to]
+    plane = [lax.rem(y + step, PLANES) for step in range(PLANES)]
 
     def others(act):
         @pl.loop(0, SIDE)
@@ -85,6 +87,7 @@
     odd_load = pltpu.make_async_copy(odd_hbm, odd, t_sem.at[1])
     for slab in range(4):
         strain_load(slab).start()
+
     even_load.start()
     odd_load.start()
 
@@ -92,77 +95,12 @@
 
     others(
         lambda a, b: pl.semaphore_signal(
-            barrier, inc=1, device_id=(y, (row_to(a) + z_to[b]) * 2 + core), device_id_type=MESH
+            barrier, inc=1, device_id=(y, row_to(a) * 2 + z_db[b]), device_id_type=MESH
         )
     )
     for step in range(1, PLANES):
         pl.semaphore_signal(barrier, inc=1, device_id=((y + step) % PLANES, d), device_id_type=MESH)
     pl.semaphore_signal(barrier, inc=1, device_id=sibling, device_id_type=MESH)
-
-    def node_copy(a, b):
-        return remote(node.at[chip], node.at[chip], nd_s, nd_r, (y, (row_to(a) + z_to[b]) * 2 + core))
-
-    def quad_copy(step):
-        return remote(node.at[:, 0:16], quads.at[y], q_s, q_r, ((y + step) % PLANES, d))
-
-    local = xin.shape[1]
-    steps = xin.shape[2]
-    quarter = steps // 4
-    rescale = steps ** (-0.5)
-    width = 256
-
-    def part_copy(part, a, b):
-        to = row_to(a) + z_to[b]
-        return remote(
-            snd.at[part, to], got.at[part, chip, core], a_s.at[part], a_r.at[part, a, b], (y, to * 2 + core)
-        )
-
-    def part_forward(part, a, b, of):
-        s = row_from(a) + z_from[b]
-        return remote(got.at[part, s, core], got.at[part, s, of], f_s.at[part], f_r.at[part, a, b], sibling)
-
-    def spectra(t):
-        @pl.loop(0, 4)
-        def _(r):
-            slab = 4 * t + r
-            pltpu.make_async_copy(fs.at[0], xin.at[slab], x_sem.at[slab]).wait()
-
-            @pl.loop(0, quarter // width)
-            def _(n):
-                at = pl.multiple_of(n * width, width)
-                x0, x1, x2, x3 = (xin[slab, :, pl.ds(at + q * quarter, width)].astype(f32) for q in range(4))
-                a, b = x0 + x2, x1 + x3
-                span = pl.ds(r * local, local)
-                fold_even[0, span, pl.ds(at, width)] = (a + b).astype(bf16)
-                fold_even[1, span, pl.ds(at, width)] = (a - b).astype(bf16)
-                fold_odd[span, pl.ds(at, width)] = (x0 - x2).astype(bf16)
-                fold_odd[span, pl.ds(at + quarter, width)] = (x1 - x3).astype(bf16)
-
-        if t < PARTS - 1:
-            for slab in range(4 * t + 4, 4 * t + 8):
-                strain_load(slab).start()
-        if t == 0:
-            even_load.wait()
-            odd_load.wait()
-        for n in range(4):
-            if n < 2:
-                sums = jnp.dot(fold_even[n], even[n], preferred_element_type=f32)
-            else:
-                sums = jnp.dot(fold_odd[...], odd[:, (n - 2) * 256 : (n - 1) * 256], preferred_element_type=f32)
-            sums = (sums * rescale).astype(bf16)
-            for u in (0, 1):
-                for r in range(4):
-                    at = 128 * (r // 2)
-                    snd[t, 4 * n + 2 * u + r % 2, :, at : at + 128] = sums[
-                        r * local : (r + 1) * local, 128 * u : 128 * u + 128
-                    ]
-
-    def depart(part):
-        others(lambda a, b: part_copy(part, a, b).start())
-        got[part, chip, core] = snd[part, chip]
-        part_forward(part, SIDE - 1, SIDE - 1, core).start()
-
-    spectra(0)
 
     points = slot.shape[2]
     nodef[...] = jnp.zeros_like(nodef)
@@ -194,6 +132,74 @@
             nodef[24 + 2 * k + q : 25 + 2 * k + q, :] = row[:, 128 * q : 128 * q + 128]
     node[chip] = nodef[...].astype(bf16)
 
+    def node_copy(a, b):
+        return remote(node.at[chip], node.at[chip], nd_s, nd_r, (y, row_to(a) * 2 + z_db[b]))
+
+    def quad_copy(step):
+        return remote(node.at[:, 0:16], quads.at[y], q_s, q_r, ((y + step) % PLANES, d))
+
+    local = xin.shape[1]
+    steps = xin.shape[2]
+    quarter = steps // 4
+    rescale = steps ** (-0.5)
+    width = 256
+
+    def part_copy(part, a, b):
+        row = row_to(a)
+        return remote(
+            snd.at[part, row + z_to[b]],
+            got.at[part, chip, core],
+            a_s.at[part],
+            a_r.at[part, a],
+            (y, row * 2 + z_db[b]),
+        )
+
+    def part_forward(part, a, of):
+        row = pl.ds(row_from(a), SIDE)
+        return remote(got.at[part, row, core], got.at[part, row, of], f_s.at[part], f_r.at[part, a], sibling)
+
+    def spectra(t):
+        @pl.loop(0, 4)
+        def _(r):
+            slab = 4 * t + r
+            pltpu.make_async_copy(fs.at[0], xin.at[slab], x_sem.at[slab]).wait()
+
+            @pl.loop(0, quarter // width)
+            def _(n):
+                at = pl.multiple_of(n * width, width)
+                x0, x1, x2, x3 = (xin[slab, :, pl.ds(at + q * quarter, width)].astype(f32) for q in range(4))
+                a, b = x0 + x2, x1 + x3
+                span = pl.ds(r * local, local)
+                fold_even[0, span, pl.ds(at, width)] = (a + b).astype(bf16)
+                fold_even[1, span, pl.ds(at, width)] = (a - b).astype(bf16)
+                fold_odd[span, pl.ds(at, width)] = (x0 - x2).astype(bf16)
+                fold_odd[span, pl.ds(at + quarter, width)] = (x1 - x3).astype(bf16)
+
+        if t < PARTS - 1:
+            for slab in range(4 * t + 4, 4 * t + 8):
+                strain_load(slab).start()
+        if t == 0:
+            even_load.wait()
+            odd_load.wait()
+        for n in range(4):
+            if n < 2:
+                sums = jnp.dot(fold_even[n], even[n], preferred_element_type=f32)
+            else:
+                sums = jnp.dot(fold_odd[...], odd[:, (n - 2) * 256 : (n - 1) * 256], preferred_element_type=f32)
+            sums = (sums * rescale).astype(bf16)
+            for u in (0, 1):
+                for r in range(4):
+                    at = 128 * (r // 2)
+                    snd[t, 4 * n + 2 * u + r % 2, :, at : at + 128] = sums[
+                        r * local : (r + 1) * local, 128 * u : 128 * u + 128
+                    ]
+
+    def depart(part):
+        others(lambda a, b: part_copy(part, a, b).start())
+        got[part, chip, core] = snd[part, chip]
+
+    spectra(0)
+
     pl.semaphore_wait(barrier, CHIPS - 1 + 1 + PLANES - 1)
 
     for step in range(1, PLANES):
@@ -227,9 +233,8 @@
     chosen = chosen * group_weight * (component_scale * count ** (-0.5))
     high = chosen.astype(bf16).astype(f32)
     low = chosen - high
-    bandx[...] = jnp.concatenate(
-        [jnp.concatenate([high, high], axis=1), jnp.concatenate([low, jnp.zeros_like(low)], axis=1)], axis=0
-    ).astype(bf16)
+    lane = lax.broadcasted_iota(i32, chosen.shape, 1)
+    bandx[...] = jnp.concatenate([high, jnp.where(lane < 64, low, 0.0)], axis=0).astype(bf16)
 
     sib_copy.wait_recv()
 
@@ -247,36 +252,28 @@
             onehot[s, 128 * q : 128 * q + 128, :] = hits.T.astype(bf16)
 
     def receive(part, a):
-        def one(b):
-            part_copy(part, a, b).wait_recv()
-            part_forward(part, a, b, core).start()
-
-        for b in range(SIDE - 1):
-            one(b)
+        def arrived(count):
+            blocks = got.at[part, 0:count, core]
+            remote(blocks, blocks, a_s.at[part], a_r.at[part, a], sibling).wait_recv()
 
         @pl.when(a < SIDE - 1)
         def _():
-            one(SIDE - 1)
+            arrived(SIDE)
+
+        @pl.when(a == SIDE - 1)
+        def _():
+            arrived(SIDE - 1)
+
+        part_forward(part, a, core).start()
 
     def gather(part, a):
-        for b in range(SIDE):
-            part_forward(part, a, b, 1 - core).wait_recv()
+        part_forward(part, a, 1 - core).wait_recv()
         for b in range(SIDE):
             s = row_from(a) + z_from[b]
             at = pl.ds(pl.multiple_of(s * 16, 16), 16)
             found = got[part, s].reshape(2 * local, 256)
             taken = jnp.dot(onehot[s], found, preferred_element_type=f32)
             rows[:, at, 256 * part : 256 * part + 256] = taken.reshape(CHIPS, 16, 256).astype(bf16)
-
-    @pl.loop(0, SIDE + 1)
-    def _(a):
-        @pl.when(a < SIDE)
-        def _():
-            receive(0, a)
-
-        @pl.when(a >= 1)
-        def _():
-            gather(0, a - 1)
 
     remote(quads.at[0:3], quads.at[0:3], q_s, q_r, sibling).wait_recv()
 
@@ -294,19 +291,33 @@
                         two, axis=0
                     ).astype(bf16)
 
+    @pl.loop(0, SIDE + 1)
+    def _(a):
+        @pl.when(a < SIDE)
+        def _():
+            receive(0, a)
+
+        @pl.when(a >= 1)
+        def _():
+            gather(0, a - 1)
+
     over_slots = (((0,), (0,)), ((), ()))
 
     def mixed(o, w, part):
         at = 256 * part + 128 * w
         return lax.dot_general(rows[o, :, at : at + 128], mix[o, w], over_slots, preferred_element_type=f32)
 
+    def halves(product):
+        return product[0:64] + product[64:128]
+
     for part in (0, 1):
+
         @pl.loop(0, SIDE)
         def _(a):
             receive(part + 1, a)
             for e in range(SIDE):
                 o = SIDE * a + e
-                product = mixed(o, 0, part) * mixed(o, 1, part)
+                product = halves(mixed(o, 0, part) * mixed(o, 1, part))
                 cross[o] = product if part == 0 else cross[o] + product
 
         @pl.loop(0, SIDE)
@@ -316,38 +327,34 @@
     pl.semaphore_wait(plane_sem, PLANES - 1)
 
     def sum_copy(a, b, step):
-        to = row_to(a) + z_to[b]
-        p = (y + step) % PLANES
-        at = (SIDE * a + b) * PLANES + step
-        return remote(rss.at[to * PLANES + p], rsr.at[at], rs_s, rs_r, (p, to * 2 + core))
-
-    @pl.loop(0, SIDE)
-    def _(a):
-        for pair in (0, 2):
-            for b in (pair, pair + 1):
-                o = row_to(a) + z_to[b]
-                total = cross[o] + mixed(o, 0, 2) * mixed(o, 1, 2)
-                high = total.astype(bf16)
-                low = (total - high.astype(f32)).astype(bf16)
-                banded = jnp.dot(bandx[...], jnp.concatenate([high, low], axis=0), preferred_element_type=f32)
-                banded = banded[0:16] + banded[16:32]
-                for p in range(PLANES):
-                    pieces = [banded[4 * p : 4 * p + 4, 128 * q : 128 * q + 128] for q in range(points // 128)]
-                    rss[o * PLANES + p] = jnp.concatenate(pieces, axis=0).astype(bf16)
-            for b in (pair, pair + 1):
-                for step in (2, 1, 3):
-                    sum_copy(a, b, step).start()
-            sum_copy(a, pair, 0).start()
-            if pair == 0:
-                sum_copy(a, 1, 0).start()
-            else:
-
-                @pl.when(a < SIDE - 1)
-                def _():
-                    sum_copy(a, 3, 0).start()
+        at = (SIDE * a + b) * PLANES
+        p = plane[step]
+        return remote(rss.at[at + p], rsr.at[at + step], rs_s, rs_r, (p, row_to(a) * 2 + z_db[b]))
+
+    def sums_two(a, pair):
+        for b in (pair, pair + 1):
+            o = row_to(a) + z_to[b]
+            total = cross[o] + halves(mixed(o, 0, 2) * mixed(o, 1, 2))
+            high = total.astype(bf16)
+            low = (total - high.astype(f32)).astype(bf16)
+            banded = jnp.dot(bandx[...], jnp.concatenate([high, low], axis=0), preferred_element_type=f32)
+            banded = banded[0:16] + banded[16:32]
+            for p in range(PLANES):
+                pieces = [banded[4 * p : 4 * p + 4, 128 * q : 128 * q + 128] for q in range(points // 128)]
+                rss[(SIDE * a + b) * PLANES + p] = jnp.concatenate(pieces, axis=0).astype(bf16)
+
+    def send_two(a, pair):
+        for b in (pair, pair + 1):
+            for step in (2, 1, 3) if (a, b) == (SIDE - 1, SIDE - 1) else (2, 1, 3, 0):
+                sum_copy(a, b, step).start()
+
+    pairs = [(a, pair) for a in range(SIDE) for pair in (0, 2)]
+    for n, (a, pair) in enumerate(pairs):
+        sums_two(a, pair)
+        send_two(a, pair)
 
     own = (CHIPS - 1) * PLANES
-    rsr[own] = rss[chip * PLANES + y]
+    rsr[own] = rss[own + y]
     remote(rss.at[0:63], rsr.at[0:63], rs_s, rs_r, sibling).wait_recv()
 
     summed = jnp.sum(rsr[...].astype(f32), axis=0)
@@ -360,8 +367,8 @@
     remote(rss.at[0:63], rsr.at[0:63], rs_s, rs_r, sibling).wait_send()
     for part in range(PARTS):
         sent, came = snd.at[part, 0:15], got.at[part, :, core]
-        remote(sent, sent, a_s.at[part], a_r.at[part, 0, 0], sibling).wait_send()
-        remote(came, came, f_s.at[part], f_r.at[part, 0, 0], sibling).wait_send()
+        remote(sent, sent, a_s.at[part], a_r.at[part, 0], sibling).wait_send()
+        remote(came, came, f_s.at[part], f_r.at[part, 0], sibling).wait_send()
 
 
 def per_device(even, odd, fwd, bwd, request, slot, weight, band, misfit, group):
@@ -403,8 +410,8 @@
             pltpu.VMEM((CHIPS, 256, 2 * local), bf16),
             pltpu.VMEM((CHIPS, 2, 256, points), bf16),
             pltpu.VMEM((CHIPS, 256, 768), bf16),
-            pltpu.VMEM((CHIPS, 128, points), f32),
-            pltpu.VMEM((2 * bands, 256), bf16),
+            pltpu.VMEM((CHIPS, 64, points), f32),
+            pltpu.VMEM((2 * bands, 128), bf16),
             pltpu.VMEM((CHIPS * PLANES, 16, 128), bf16),
             pltpu.VMEM((CHIPS * PLANES, 16, 128), bf16),
             dma((12,)),
@@ -414,9 +421,9 @@
             dma,
             dma,
             dma((PARTS,)),
-            dma((PARTS, SIDE, SIDE)),
+            dma((PARTS, SIDE)),
             dma((PARTS,)),
-            dma((PARTS, SIDE, SIDE)),
+            dma((PARTS, SIDE)),
             dma,
             dma,
             dma,

time: 48.4 us -> 47.4 us (0.979)
  Pallas kernels: 46.8 us -> 45.9 us
    pallas_call x1, Pallas kernels: 46.8 us -> 45.9 us  [per_device(): pl.pallas_call(body, out_shape=jax.ShapeDtypeStruct((bands // 4, points),...]
where the time goes in v2:
time: 47.4 us; the launch traced here: 47.2 us
  Pallas kernels  45.9 us (97%)
  local copies, waits for them, and re-layouts  1.3 us (3%)
    pallas_call x1, Pallas kernels, per_device(): pl.pallas_call(body, out_shape=jax.ShapeDtypeStruct((bands // 4, points),...  45.9 us
    unnamed x1, local copies, waits for them, and re-layouts  1.3 us

profile of v2, /device:TPU:1, one launch (start us, length us, event | category | flops | bytes accessed | tf_op | source)
XLA Modules:
  0.0 47.2 jit_solution(17026583542253081384)
XLA Ops:
  0.0 45.9 %shard_map.100 = f32[4,512]{1,0:T(4,128)} custom-call(bf16[6,64,8192]{2,1,0:T(8,128)(2,1)} %bitcast.11, bf16[6,64,8192]{2,1,0:T(8,128)(2,1)} %bitcast.12, bf16[2,2048,256]{2,1,0:T(8,128)(2,1)} %constant.4.clone.even_hbm, bf16[4096,512]{1,0:T(8,128)(2,1)} %constant.5.clone.odd_hbm, s32[2,8,512]{2,1,0:T(8,128)} %slot.1, f32[2,8,512]{2,1,0:T(8,128)} %weight.1, ...), custom_call_target="tpu_custom_call" | custom-call | tf_op jit(solution)/shard_map/pallas_call | solution.py:393
  45.9 1.3 %copy.12 = f32[4,512]{1,0:T(4,128)} copy(f32[4,512]{1,0:T(4,128)} %shard_map.100) | data formatting | bytes 16384

commit v3 on v2

--- a/solution.py
+++ b/solution.py
@@ -238,7 +238,7 @@
 
     sib_copy.wait_recv()
 
-    @pl.loop(0, CHIPS)
+    @pl.loop(0, CHIPS, unroll=4)
     def _(s):
         mine = node[s, 16:32].astype(f32)
         theirs = sib[s].astype(f32)

time: 47.4 us -> 47.4 us (level)
  no operation moved by 1% of the time
where the time goes in v3:
time: 47.4 us; the launch traced here: 47.2 us
  Pallas kernels  45.9 us (97%)
  local copies, waits for them, and re-layouts  1.3 us (3%)
    pallas_call x1, Pallas kernels, per_device(): pl.pallas_call(body, out_shape=jax.ShapeDtypeStruct((bands // 4, points),...  45.9 us
    unnamed x1, local copies, waits for them, and re-layouts  1.3 us

profile of v3, /device:TPU:1, one launch (start us, length us, event | category | flops | bytes accessed | tf_op | source)
XLA Modules:
  0.0 47.2 jit_solution(4463230725890632715)
XLA Ops:
  0.0 45.9 %shard_map.100 = f32[4,512]{1,0:T(4,128)} custom-call(bf16[6,64,8192]{2,1,0:T(8,128)(2,1)} %bitcast.11, bf16[6,64,8192]{2,1,0:T(8,128)(2,1)} %bitcast.12, bf16[2,2048,256]{2,1,0:T(8,128)(2,1)} %constant.4.clone.even_hbm, bf16[4096,512]{1,0:T(8,128)(2,1)} %constant.5.clone.odd_hbm, s32[2,8,512]{2,1,0:T(8,128)} %slot.1, f32[2,8,512]{2,1,0:T(8,128)} %weight.1, ...), custom_call_target="tpu_custom_call" | custom-call | tf_op jit(solution)/shard_map/pallas_call | solution.py:393
  45.9 1.3 %copy.12 = f32[4,512]{1,0:T(4,128)} copy(f32[4,512]{1,0:T(4,128)} %shard_map.100) | data formatting | bytes 16384
